TPU v7x, 512 devices: a whole 4x4x16 slice. The times are simulated.
512 devices in a mesh: dp: 2 (over core), seq: 16 (over y, x), head: 16 (over z).
Axes of the slice: x: 4, y: 4, z: 16, core: 2. Of those that a mesh axis runs over, the one named last changes fastest.
Arguments:
- queries: bfloat16 [65536, 32, 128], P(('dp', 'seq', 'head')), parts along dimension 0, may hold values from -6 to 6
- keys: bfloat16 [65536, 4, 128], P(('dp', 'seq', 'head')), parts along dimension 0, may hold values from -6 to 6
- values: bfloat16 [65536, 4, 128], P(('dp', 'seq', 'head')), parts along dimension 0, may hold values from -6 to 6
- out_grad: bfloat16 [65536, 32, 128], P(('dp', 'seq', 'head')), parts along dimension 0, may hold values from -24 to 24
- kept_blocks: int32 [4, 256, 1], replicated, may hold values from 0 to 255, as said below
- sink_blocks: int32 [4], replicated, may hold values from 1 to 3
- window_blocks: int32 [4], replicated, may hold values from 2 to 4
Outputs:
- grad_queries: bfloat16 [65536, 32, 128], P(('dp', 'seq', 'head')), parts along dimension 0
- grad_keys: bfloat16 [65536, 4, 128], P(('dp', 'seq', 'head')), parts along dimension 0
- grad_values: bfloat16 [65536, 4, 128], P(('dp', 'seq', 'head')), parts along dimension 0
There are 2 independent parts, one for each index of `dp`. A program takes and returns all parts, laid end to end along the dimension named above; an argument that names none is the same for every part. Nothing has to cross between parts.
Inputs may be any that keep to these rules, and one draw needn't show every extreme that they name: `kept_blocks`: entries that name a block after the query block are ignored; entries may name sink or window blocks. For each key head and each index of seq, the 16 entries of that index's query blocks name blocks held by one index of seq at most 2 times in all, and exactly 2 times for some index of seq.
All inputs are finite; a program needn't handle non-finite values.
Results may differ from a plain program's by a relative error of at most 0.0076.
Values may be sent and summed in bfloat16 or wider, within the bound.
A program may use at most 128 MiB of HBM per device.

v0:
```python
import math
import jax
import jax.numpy as jnp
import numpy as np
from jax import lax
from jax.sharding import PartitionSpec as P

BLK = 128
SINK_MOST = 3
WIN_MOST = 4


def spread(array, axis, root):
    mine = lax.axis_index(axis) == root
    return lax.psum(jnp.where(mine, array, jnp.zeros_like(array)), axis)


def shifted(block, axis, distance):
    devices = range(lax.axis_size(axis))
    route = [(i - distance, i) for i in devices if i - distance in devices]
    return lax.ppermute(block, axis, route)


def slot_table(query_blocks, kept_rows, sink_count, window_count):
    current = query_blocks[:, None]
    number = query_blocks.shape[0]
    sink_ids = jnp.broadcast_to(
        jnp.arange(SINK_MOST, dtype=jnp.int32)[None, :], (number, SINK_MOST)
    )
    sink_ok = (sink_ids < sink_count) & (sink_ids <= current) & (current - sink_ids >= window_count)
    offsets = jnp.arange(WIN_MOST, dtype=jnp.int32)[None, :]
    window_ids = current - offsets
    window_ok = (offsets < window_count) & (window_ids >= 0)
    kept_ok = (
        (kept_rows <= current) & (kept_rows >= sink_count) & (current - kept_rows >= window_count)
    )
    repeated = jnp.zeros((number,), dtype=bool)
    fresh = [jnp.logical_not(repeated)]
    kept_ok = kept_ok & jnp.stack(fresh, axis=1)
    slot_ids = jnp.concatenate([sink_ids, window_ids, kept_rows], axis=1)
    slot_ok = jnp.concatenate([sink_ok, window_ok, kept_ok], axis=1)
    return (jnp.maximum(slot_ids, 0), slot_ok)


def slot_mask(slot_ok):
    number, slots = slot_ok.shape
    within = jnp.arange(BLK, dtype=jnp.int32)
    diagonal = within[None, :] <= within[:, None]
    on_diagonal = jnp.arange(slots, dtype=jnp.int32) == SINK_MOST
    allowed = slot_ok[:, None, :, None] & (
        jnp.logical_not(on_diagonal)[None, None, :, None] | diagonal[None, :, None, :]
    )
    return allowed.reshape(number, BLK, slots * BLK)


def body(queries, keys, values, out_grad, kept_blocks, sink_blocks, window_blocks):
    head_count = lax.axis_size("head")
    seq_count = lax.axis_size("seq")
    seq_index = lax.axis_index("seq")
    head_index = lax.axis_index("head")
    kv_total = keys.shape[1]
    repeat = head_count // kv_total
    keys_wide = jnp.repeat(keys, repeat, axis=1)
    values_wide = jnp.repeat(values, repeat, axis=1)
    q_local, k_local, v_local, grad_local = (
        lax.all_to_all(queries, "head", split_axis=1, concat_axis=0, tiled=True),
        lax.all_to_all(keys_wide, "head", split_axis=1, concat_axis=0, tiled=True),
        lax.all_to_all(values_wide, "head", split_axis=1, concat_axis=0, tiled=True),
        lax.all_to_all(out_grad, "head", split_axis=1, concat_axis=0, tiled=True),
    )
    seq_rows, heads_here, width = q_local.shape
    local_blocks = seq_rows // BLK
    scale = 1.0 / math.sqrt(width)
    kv_pairs = jnp.concatenate([k_local[:, 0], v_local[:, 0]], axis=1)
    pair_blocks = kv_pairs.reshape(local_blocks, BLK, 2 * width)
    sink_pairs = spread(kv_pairs[: SINK_MOST * BLK], "seq", 0).reshape(SINK_MOST, BLK, 2 * width)
    reach = WIN_MOST - 1
    before = shifted(kv_pairs[seq_rows - reach * BLK :], "seq", 1)
    extended = jnp.concatenate([before, kv_pairs], axis=0).reshape(
        local_blocks + reach, BLK, 2 * width
    )
    kv_head = head_index // repeat
    head_lists = lax.dynamic_index_in_dim(kept_blocks, kv_head, 0, keepdims=False)
    sink_count = lax.dynamic_index_in_dim(sink_blocks, kv_head, 0, keepdims=False)
    window_count = lax.dynamic_index_in_dim(window_blocks, kv_head, 0, keepdims=False)
    keep = head_lists.shape[1]
    entries = local_blocks * keep
    capacity = max(2, -(-entries // seq_count))
    all_lists = head_lists.reshape(seq_count, entries)
    owners = all_lists // local_blocks
    order = jnp.arange(entries, dtype=jnp.int32)
    earlier_mask = order[None, :] < order[:, None]
    ranks = jnp.sum(
        ((owners[:, :, None] == owners[:, None, :]) & earlier_mask[None]).astype(jnp.int32), axis=2
    )
    place_ids = jnp.arange(capacity, dtype=jnp.int32)
    sent_match = (owners[:, None, :] == seq_index) & (ranks[:, None, :] == place_ids[None, :, None])
    sent_block = jnp.sum(
        jnp.where(sent_match, all_lists[:, None, :] - seq_index * local_blocks, 0), axis=2
    )
    outgoing = pair_blocks[sent_block]
    incoming = lax.all_to_all(outgoing, "seq", split_axis=0, concat_axis=0, tiled=True)
    my_lists = lax.dynamic_index_in_dim(all_lists, seq_index, 0, keepdims=False)
    my_owners = my_lists // local_blocks
    my_ranks = lax.dynamic_index_in_dim(ranks, seq_index, 0, keepdims=False)
    far_pairs = incoming.reshape(seq_count * capacity, BLK, 2 * width)[
        my_owners * capacity + my_ranks
    ]
    query_blocks = seq_index * local_blocks + jnp.arange(local_blocks, dtype=jnp.int32)
    unused_ids, slot_ok = slot_table(
        query_blocks, my_lists.reshape(local_blocks, keep), sink_count, window_count
    )
    allowed = slot_mask(slot_ok)
    slots = SINK_MOST + WIN_MOST + keep
    span = 2
    turns = local_blocks // span
    window_index = np.array(
        [[row + reach - offset for offset in range(WIN_MOST)] for row in range(span)],
        dtype=np.int32,
    )

    def turn(carry, inputs):
        near_sum, sink_sum = carry
        position, q_part, g_part, mask_part, far_part = inputs
        window_part = lax.dynamic_slice_in_dim(extended, position * span, span + reach, 0)
        window_slots = window_part[window_index]
        sink_slots = jnp.broadcast_to(sink_pairs[None], (span,) + sink_pairs.shape)
        gathered = jnp.concatenate([sink_slots, window_slots, far_part], axis=1).reshape(
            span, slots * BLK, 2 * width
        )
        key_part = gathered[..., :width]
        value_part = gathered[..., width:]
        scores = (
            jnp.einsum("bthd,bud->bhtu", q_part, key_part, preferred_element_type=jnp.float32)
            * scale
        )
        scores = jnp.where(mask_part[:, None], scores, -jnp.inf)
        top = jnp.max(scores, axis=3, keepdims=True)
        lse = top + jnp.log(jnp.sum(jnp.exp(scores - top), axis=3, keepdims=True))
        probs = jnp.exp(scores - lse)
        probs_low = probs.astype(jnp.bfloat16)
        dprobs = jnp.einsum(
            "bthd,bud->bhtu", g_part, value_part, preferred_element_type=jnp.float32
        )
        delta = jnp.sum(probs * dprobs, axis=3, keepdims=True)
        dscores = (probs * (dprobs - delta)).astype(jnp.bfloat16)
        grad_q = (
            jnp.einsum("bhtu,bud->bthd", dscores, key_part, preferred_element_type=jnp.float32)
            * scale
        ).astype(jnp.bfloat16)
        key_terms = (
            jnp.einsum("bhtu,bthd->bud", dscores, q_part, preferred_element_type=jnp.float32)
            * scale
        )
        value_terms = jnp.einsum(
            "bhtu,bthd->bud", probs_low, g_part, preferred_element_type=jnp.float32
        )
        terms = jnp.concatenate([key_terms, value_terms], axis=2).reshape(
            span, slots, BLK, 2 * width
        )
        sink_sum = sink_sum + jnp.sum(terms[:, :SINK_MOST], axis=0)
        window_terms = terms[:, SINK_MOST : SINK_MOST + WIN_MOST]
        placed = (
            jnp.zeros((span + reach, BLK, 2 * width), jnp.float32)
            .at[window_index]
            .add(window_terms)
        )
        previous = lax.dynamic_slice_in_dim(near_sum, position * span, span + reach, 0)
        near_sum = lax.dynamic_update_slice_in_dim(near_sum, previous + placed, position * span, 0)
        return ((near_sum, sink_sum), (grad_q, terms[:, SINK_MOST + WIN_MOST :]))

    start = (
        jnp.zeros((local_blocks + reach, BLK, 2 * width), jnp.float32),
        jnp.zeros((SINK_MOST, BLK, 2 * width), jnp.float32),
    )
    scan_inputs = (
        jnp.arange(turns, dtype=jnp.int32),
        q_local.reshape(turns, span, BLK, heads_here, width),
        grad_local.reshape(turns, span, BLK, heads_here, width),
        allowed.reshape(turns, span, BLK, slots * BLK),
        far_pairs.reshape(turns, span, keep, BLK, 2 * width),
    )
    (near_sum, sink_sum), (grad_blocks, far_terms) = lax.scan(turn, start, scan_inputs)
    grad_rows = grad_blocks.reshape(seq_rows, heads_here, width)
    grad_queries = lax.all_to_all(grad_rows, "head", split_axis=0, concat_axis=1, tiled=True)
    far_terms = far_terms.reshape(entries, BLK, 2 * width)
    owner_ids = jnp.arange(seq_count, dtype=jnp.int32)
    back_match = (my_owners[None, None, :] == owner_ids[:, None, None]) & (
        my_ranks[None, None, :] == place_ids[None, :, None]
    )
    outbound = jnp.einsum(
        "ocp,pbd->ocbd", back_match.astype(jnp.float32), far_terms, precision=lax.Precision.HIGHEST
    )
    sent_valid = jnp.any(sent_match, axis=2)
    owner_hits = (
        (sent_block[:, :, None] == jnp.arange(local_blocks, dtype=jnp.int32)[None, None, :])
        & sent_valid[:, :, None]
    ).astype(jnp.float32)
    arrived = lax.all_to_all(outbound, "seq", split_axis=0, concat_axis=0, tiled=True)
    far_added = jnp.einsum("rcb,rctd->btd", owner_hits, arrived, precision=lax.Precision.HIGHEST)
    spill = shifted(near_sum[:reach], "seq", -1)
    sink_total = lax.psum(sink_sum, "seq")
    own = near_sum[reach:] + far_added
    own = own + jnp.concatenate(
        [jnp.zeros((local_blocks - reach, BLK, 2 * width), jnp.float32), spill], axis=0
    )
    sink_share = jnp.where(seq_index == 0, sink_total, jnp.zeros_like(sink_total))
    own = own + jnp.concatenate(
        [sink_share, jnp.zeros((local_blocks - SINK_MOST, BLK, 2 * width), jnp.float32)], axis=0
    )
    flat = own.reshape(seq_rows, 1, 2 * width)
    returned = lax.all_to_all(flat, "head", split_axis=0, concat_axis=1, tiled=True)
    tok_rows = returned.shape[0]
    combined = jnp.sum(returned.reshape(tok_rows, kv_total, repeat, 2 * width), axis=2)
    grad_keys = combined[..., :width].astype(jnp.bfloat16)
    grad_values = combined[..., width:].astype(jnp.bfloat16)
    return (grad_queries, grad_keys, grad_values)


def solution(mesh):
    placed = (
        P(("dp", "seq", "head"), None, None),
        P(("dp", "seq", "head"), None, None),
        P(("dp", "seq", "head"), None, None),
        P(("dp", "seq", "head"), None, None),
        P(),
        P(),
        P(),
    )
    return jax.shard_map(
        body,
        mesh=mesh,
        in_specs=placed,
        out_specs=(
            P(("dp", "seq", "head"), None, None),
            P(("dp", "seq", "head"), None, None),
            P(("dp", "seq", "head"), None, None),
        ),
        check_vma=False,
    )
```

profile of v0, /device:TPU:32, one launch (start us, length us, event | category | flops | bytes accessed | tf_op | source)
XLA Modules:
  0.0 896.1 jit_solution(6246537948425911620)
XLA Ops:
  9.0 15.2 %all-to-all-start = ((bf16[128,16,128]{2,0,1:T(8,128)(2,1)}), bf16[128,16,128]{2,0,1:T(8,128)(2,1)S(1)}, u32[]{:S(2)}, u32[]{:S(2)}) async-start(bf16[128,16,128]{2,0,1:T(8,128)(2,1)} %bitcast.5), calls=%async_computation | async-start | bytes 1048576 | tf_op jit(solution)/shard_map/all_to_all | solution.py:67
  25.1 27.3 %all-to-all-done = bf16[128,16,128]{2,0,1:T(8,128)(2,1)S(1)} async-done(((bf16[128,16,128]{2,0,1:T(8,128)(2,1)}), bf16[128,16,128]{2,0,1:T(8,128)(2,1)S(1)}, u32[]{:S(2)}, u32[]{:S(2)}) %all-to-all-start) | async-done | bytes 524320 | tf_op jit(solution)/shard_map/all_to_all | solution.py:67
  53.4 7.2 all-to-all-start.1
  61.4 27.4 %all-to-all-done.1 = bf16[128,16,128]{2,0,1:T(8,128)(2,1)S(1)} async-done(((bf16[128,16,128]{2,0,1:T(8,128)(2,1)}), bf16[128,16,128]{2,0,1:T(8,128)(2,1)S(1)}, u32[]{:S(2)}, u32[]{:S(2)}) %all-to-all-start.1) | async-done | bytes 524320 | tf_op jit(solution)/shard_map/all_to_all | solution.py:68
  88.9 2.0 gather_fusion.1
  91.0 7.2 all-to-all-start.2
  99.6 25.4 %all-to-all-done.2 = bf16[16,2,128,256]{3,2,1,0:T(8,128)(2,1)} async-done(((bf16[16,2,128,256]{3,2,1,0:T(8,128)(2,1)}), bf16[16,2,128,256]{3,2,1,0:T(8,128)(2,1)}, u32[]{:S(2)}, u32[]{:S(2)}) %all-to-all-start.2) | async-done | bytes 2097184 | tf_op jit(solution)/shard_map/all_to_all | solution.py:102
  125.0 12.1 %all-to-all-start.3 = ((bf16[128,32,128]{2,0,1:T(8,128)(2,1)}), bf16[128,32,128]{2,0,1:T(8,128)(2,1)}, u32[]{:S(2)}, u32[]{:S(2)}) async-start(bf16[128,32,128]{2,0,1:T(8,128)(2,1)} %copy.112), calls=%async_computation.3 | async-start | bytes 2097152 | tf_op jit(solution)/shard_map/all_to_all | solution.py:66
  138.6 45.9 %all-to-all-done.3 = bf16[128,32,128]{2,0,1:T(8,128)(2,1)} async-done(((bf16[128,32,128]{2,0,1:T(8,128)(2,1)}), bf16[128,32,128]{2,0,1:T(8,128)(2,1)}, u32[]{:S(2)}, u32[]{:S(2)}) %all-to-all-start.3) | async-done | bytes 1048608 | tf_op jit(solution)/shard_map/all_to_all | solution.py:66
  184.5 9.5 %all-to-all-start.4 = ((bf16[128,32,128]{2,0,1:T(8,128)(2,1)}), bf16[128,32,128]{2,0,1:T(8,128)(2,1)}, u32[]{:S(2)}, u32[]{:S(2)}) async-start(bf16[128,32,128]{2,0,1:T(8,128)(2,1)} %copy.113), calls=%async_computation.4 | async-start | bytes 2097152 | tf_op jit(solution)/shard_map/all_to_all | solution.py:69
  200.1 4.7 broadcast_and_fusion
  207.6 3.2 collective-permute-done
  211.0 3.2 gather_fusion.2
  214.2 108.9 %all-reduce.5.cloned.1.call-done = bf16[384,256]{1,0:T(8,128)(2,1)} async-done(((bf16[384,256]{1,0:T(8,128)(2,1)}), bf16[384,256]{1,0:T(8,128)(2,1)}) %all-reduce.5.cloned.1.call-update) | async-done | bytes 196624 | tf_op jit(solution)/shard_map/psum | solution.py:15
  324.8 233.6 %while.19 = (s32[]{:T(128)}, f32[19,128,256]{2,1,0:T(8,128)}, f32[3,128,256]{1,0,2:T(4,128)}, bf16[8,2,128,2,128]{4,2,1,0,3:T(8,128)(2,1)}, f32[8,2,1,128,256]{3...) while((s32[]{:T(128)}, f32[19,128,256]{2,1,0:T(8,128)}, ...), condition=%wide.region_9.10_spmd.clone.clone.clone, body=%wide.region_3.9_spmd.sunk.clone.clone.clone.sunk | while | flops 680951808 | bytes 64059104 | solution.py:183
  337.3 2.5 copy.158
  339.8 2.0 constant_dynamic-slice_fusion.6
  341.9 3.7 scatter_fusion
  349.5 2.1 select_add_fusion.2
  366.3 2.5 copy.158
  368.9 2.0 constant_dynamic-slice_fusion.6
  370.9 3.7 scatter_fusion
  374.6 2.0 constant_dynamic-update-slice_fusion.6
  378.6 2.3 select_add_fusion.2
  395.6 2.5 copy.158
  398.1 2.0 constant_dynamic-slice_fusion.6
  400.1 3.7 scatter_fusion
  403.8 2.0 constant_dynamic-update-slice_fusion.6
  407.8 2.3 select_add_fusion.2
  424.8 2.5 copy.158
  427.3 2.0 constant_dynamic-slice_fusion.6
  429.4 3.7 scatter_fusion
  433.0 2.0 constant_dynamic-update-slice_fusion.6
  437.0 2.3 select_add_fusion.2
  454.0 2.5 copy.158
  456.5 2.0 constant_dynamic-slice_fusion.6
  458.6 3.7 scatter_fusion
  466.2 2.3 select_add_fusion.2
  483.2 2.5 copy.158
  485.7 2.0 constant_dynamic-slice_fusion.6
  487.8 3.7 scatter_fusion
  491.4 2.0 constant_dynamic-update-slice_fusion.6
  495.5 2.3 select_add_fusion.2
  512.4 2.5 copy.158
  515.0 2.0 constant_dynamic-slice_fusion.6
  517.0 3.7 scatter_fusion
  520.7 2.0 constant_dynamic-update-slice_fusion.6
  524.7 2.3 select_add_fusion.2
  541.6 2.5 copy.158
  544.2 2.0 constant_dynamic-slice_fusion.6
  546.2 3.7 scatter_fusion
  549.9 2.0 constant_dynamic-update-slice_fusion.6
  553.9 2.3 select_add_fusion.2
  558.4 2.2 copy.119
  562.5 5.3 copy.120
  567.8 5.2 all-to-all-start.6
  573.0 9.5 %copy.115 = bf16[2048,2,128]{2,1,0:T(2,128)(2,1)} copy(bf16[2048,2,128]{2,0,1:T(8,128)(2,1)S(1)} %bitcast.244) | data formatting | bytes 2097152 | tf_op jit(solution)/shard_map/reshape | solution.py:184
  582.5 50.3 %all-to-all-done.6 = f32[16,2,128,256]{3,1,2,0:T(2,128)} async-done(((f32[16,2,128,256]{3,1,2,0:T(2,128)}), f32[16,2,128,256]{3,1,2,0:T(2,128)}, u32[]{:S(2)}, u32[]{:S(2)}) %all-to-all-start.6) | async-done | bytes 4194336 | tf_op jit(solution)/shard_map/all_to_all | solution.py:199
  632.8 12.7 %all-to-all-start.5 = ((bf16[2048,2,128]{2,1,0:T(2,128)(2,1)}), bf16[2048,2,128]{2,1,0:T(2,128)(2,1)}, u32[]{:S(2)}, u32[]{:S(2)}) async-start(bf16[2048,2,128]{2,1,0:T(2,128)(2,1)} %copy.115), calls=%async_computation.5 | async-start | bytes 2097152 | tf_op jit(solution)/shard_map/all_to_all | solution.py:185
  651.5 111.6 %all-reduce.7.cloned.1.call-done = f32[3,128,256]{2,0,1:T(4,128)} async-done(((f32[3,128,256]{2,0,1:T(4,128)}), f32[3,128,256]{2,0,1:T(4,128)}) %all-reduce.7.cloned.1.call-update) | async-done | bytes 393232 | tf_op jit(solution)/shard_map/psum | solution.py:202
  764.3 7.5 fusion.25
  773.0 10.0 %copy.125 = f32[2048,1,256]{2,1,0:T(1,128)} copy(f32[2048,1,256]{2,0,1:T(8,128)S(1)} %bitcast.231) | data formatting | bytes 4194304 | tf_op jit(solution)/shard_map/reshape | solution.py:211
  783.0 12.7 %all-to-all-start.7 = ((f32[2048,1,256]{2,1,0:T(1,128)}), f32[2048,1,256]{2,1,0:T(1,128)S(1)}, u32[]{:S(2)}, u32[]{:S(2)}) async-start(f32[2048,1,256]{2,1,0:T(1,128)} %copy.125), calls=%async_computation.7 | async-start | bytes 4194304 | tf_op jit(solution)/shard_map/all_to_all | solution.py:212
  798.8 88.6 %all-to-all-done.7 = f32[2048,1,256]{2,1,0:T(1,128)S(1)} async-done(((f32[2048,1,256]{2,1,0:T(1,128)}), f32[2048,1,256]{2,1,0:T(1,128)S(1)}, u32[]{:S(2)}, u32[]{:S(2)}) %all-to-all-start.7) | async-done | bytes 2097184 | tf_op jit(solution)/shard_map/all_to_all | solution.py:212
  (380 shorter events, 164.7 us)
Async XLA Ops:
  7.2 53.4 %copy-start = (s32[4,256,1]{1,2,0:T(1,128)S(1)}, s32[4,256,1]{1,2,0:T(1,128)}, u32[]{:S(2)}) copy-start(s32[4,256,1]{1,2,0:T(1,128)} %param.16) | copy-start | bytes 12292
  9.0 43.4 %all-to-all-start = ((bf16[128,16,128]{2,0,1:T(8,128)(2,1)}), bf16[128,16,128]{2,0,1:T(8,128)(2,1)S(1)}, u32[]{:S(2)}, u32[]{:S(2)}) async-start(bf16[128,16,128]{2,0,1:T(8,128)(2,1)} %bitcast.5), calls=%async_computation | async-start | bytes 1048576 | tf_op jit(solution)/shard_map/all_to_all | solution.py:67
  53.4 35.4 %all-to-all-start.1 = ((bf16[128,16,128]{2,0,1:T(8,128)(2,1)}), bf16[128,16,128]{2,0,1:T(8,128)(2,1)S(1)}, u32[]{:S(2)}, u32[]{:S(2)}) async-start(bf16[128,16,128]{2,0,1:T(8,128)(2,1)} %bitcast.9), calls=%async_computation.1 | async-start | bytes 1048576 | tf_op jit(solution)/shard_map/all_to_all | solution.py:68
  61.2 29.7 %copy-start.15 = (s32[16,2]{0,1:T(2,128)}, s32[16,2]{0,1:T(2,128)S(1)}, u32[]{:S(2)}) copy-start(s32[16,2]{0,1:T(2,128)S(1)} %select_reduce_fusion) | copy-start | bytes 388
  91.0 7.2 copy-start.9
  91.0 34.1 %all-to-all-start.2 = ((bf16[16,2,128,256]{3,2,1,0:T(8,128)(2,1)}), bf16[16,2,128,256]{3,2,1,0:T(8,128)(2,1)}, u32[]{:S(2)}, u32[]{:S(2)}) async-start(bf16[16,2,128,256]{3,2,1,0:T(8,128)(2,1)} %bitcast.19), calls=%async_computation.2 | async-start | bytes 4194304 | tf_op jit(solution)/shard_map/all_to_all | solution.py:102
  98.2 39.0 %copy-start.10 = (bf16[128,32,128]{2,1,0:T(8,128)(2,1)S(1)}, bf16[128,32,128]{2,1,0:T(8,128)(2,1)}, u32[]{:S(2)}) copy-start(bf16[128,32,128]{2,1,0:T(8,128)(2,1)} %param.15) | copy-start | bytes 3145732
  125.0 59.5 %all-to-all-start.3 = ((bf16[128,32,128]{2,0,1:T(8,128)(2,1)}), bf16[128,32,128]{2,0,1:T(8,128)(2,1)}, u32[]{:S(2)}, u32[]{:S(2)}) async-start(bf16[128,32,128]{2,0,1:T(8,128)(2,1)} %copy.112), calls=%async_computation.3 | async-start | bytes 2097152 | tf_op jit(solution)/shard_map/all_to_all | solution.py:66
  137.2 56.9 %copy-start.19 = (s32[4]{0:T(128)S(1)}, s32[4]{0:T(128)}, u32[]{:S(2)}) copy-start(s32[4]{0:T(128)} %param.17) | copy-start | bytes 52
  137.2 57.6 %copy-start.20 = (s32[4]{0:T(128)S(1)}, s32[4]{0:T(128)}, u32[]{:S(2)}) copy-start(s32[4]{0:T(128)} %param.18) | copy-start | bytes 52
  184.5 138.6 %all-to-all-start.4 = ((bf16[128,32,128]{2,0,1:T(8,128)(2,1)}), bf16[128,32,128]{2,0,1:T(8,128)(2,1)}, u32[]{:S(2)}, u32[]{:S(2)}) async-start(bf16[128,32,128]{2,0,1:T(8,128)(2,1)} %copy.113), calls=%async_computation.4 | async-start | bytes 2097152 | tf_op jit(solution)/shard_map/all_to_all | solution.py:69
  194.0 129.0 %all-reduce.5.cloned.1.call-start = ((), (), s32[]{:S(2)}) async-start(), calls=%async_computation.8 | async-start | bytes 393216 | tf_op jit(solution)/shard_map/psum | solution.py:15
  205.5 5.3 collective-permute-start
  211.0 113.9 %copy-start.12 = (s32[8]{0:T(128)S(1)}, s32[8]{0:T(128)}, u32[]{:S(2)}) copy-start(s32[8]{0:T(128)} %constant.226) | copy-start | bytes 100
  323.1 1.7 copy-start.8
  324.8 1.4 copy-start.21
  324.8 3.1 copy-start.6
  327.9 2.9 copy-start.2
  349.5 4.4 copy-start.7
  349.5 4.4 copy-start.22
  353.9 3.1 copy-start.6
  357.0 2.9 copy-start.2
  378.6 4.5 copy-start.7
  378.6 4.5 copy-start.22
  383.1 3.1 copy-start.6
  386.2 2.9 copy-start.2
  407.8 4.5 copy-start.7
  407.8 4.5 copy-start.22
  412.3 3.1 copy-start.6
  415.4 2.9 copy-start.2
  437.0 4.5 copy-start.7
  437.0 4.5 copy-start.22
  441.6 3.1 copy-start.6
  444.6 2.9 copy-start.2
  466.2 4.5 copy-start.7
  466.2 4.5 copy-start.22
  470.7 1.4 copy-start.21
  470.7 3.1 copy-start.6
  473.8 2.9 copy-start.2
  495.5 4.5 copy-start.7
  495.5 4.5 copy-start.22
  500.0 3.1 copy-start.6
  503.1 2.9 copy-start.2
  524.7 4.5 copy-start.7
  524.7 4.5 copy-start.22
  529.2 1.4 copy-start.21
  529.2 3.1 copy-start.6
  532.3 2.9 copy-start.2
  553.9 4.5 copy-start.7
  553.9 4.5 copy-start.22
  558.4 2.3 copy-start.17
  558.4 2.3 copy-start.18
  567.8 5.2 copy-start.11
  567.8 65.0 %all-to-all-start.6 = ((f32[16,2,128,256]{3,1,2,0:T(2,128)}), f32[16,2,128,256]{3,1,2,0:T(2,128)}, u32[]{:S(2)}, u32[]{:S(2)}) async-start(f32[16,2,128,256]{3,1,2,0:T(2,128)} %copy.120), calls=%async_computation.6 | async-start | bytes 8388608 | tf_op jit(solution)/shard_map/all_to_all | solution.py:199
  573.0 72.5 %copy-start.4 = (f32[3,128,256]{1,0,2:T(4,128)S(1)}, f32[3,128,256]{1,0,2:T(4,128)}, u32[]{:S(2)}) copy-start(f32[3,128,256]{1,0,2:T(4,128)} %get-tuple-element.86) | copy-start | bytes 1179652
  582.5 64.1 %copy-start.3 = (f32[19,128,256]{2,1,0:T(8,128)S(1)}, f32[19,128,256]{2,1,0:T(8,128)}, u32[]{:S(2)}) copy-start(f32[19,128,256]{2,1,0:T(8,128)} %get-tuple-element.84) | copy-start | bytes 7471108
  632.8 150.2 %all-to-all-start.5 = ((bf16[2048,2,128]{2,1,0:T(2,128)(2,1)}), bf16[2048,2,128]{2,1,0:T(2,128)(2,1)}, u32[]{:S(2)}, u32[]{:S(2)}) async-start(bf16[2048,2,128]{2,1,0:T(2,128)(2,1)} %copy.115), calls=%async_computation.5 | async-start | bytes 2097152 | tf_op jit(solution)/shard_map/all_to_all | solution.py:185
  645.5 117.7 %all-reduce.7.cloned.1.call-start = ((), (), s32[]{:S(2)}) async-start(), calls=%async_computation.9 | async-start | bytes 1048576 | tf_op jit(solution)/shard_map/psum | solution.py:202
  646.6 4.8 copy-start.14
  648.1 1.6 copy-start.5
  649.7 114.6 %copy-start.16 = (s32[16,2]{0,1:T(2,128)S(1)}, s32[16,2]{0,1:T(2,128)}, u32[]{:S(2)}) copy-start(s32[16,2]{0,1:T(2,128)} %copy-done.15) | copy-start | bytes 388
  649.8 114.5 %collective-permute-start.1 = (f32[3,128,256]{2,0,1:T(4,128)S(1)}, f32[3,128,256]{2,0,1:T(4,128)S(1)}, u32[]{:S(2)}, u32[]{:S(2)}) collective-permute-start(f32[3,128,256]{2,0,1:T(4,128)S(1)} %slice.73), channel_id=1, source_target_pairs={{16,0},{32,16},{48,32},{64,48},{80,64},{96,80},{112,96},{128,112},... | collective-permute-start | bytes 1179656 | tf_op jit(solution)/shard_map/ppermute | solution.py:21
  783.0 104.4 %all-to-all-start.7 = ((f32[2048,1,256]{2,1,0:T(1,128)}), f32[2048,1,256]{2,1,0:T(1,128)S(1)}, u32[]{:S(2)}, u32[]{:S(2)}) async-start(f32[2048,1,256]{2,1,0:T(1,128)} %copy.125), calls=%async_computation.7 | async-start | bytes 4194304 | tf_op jit(solution)/shard_map/all_to_all | solution.py:212
  887.4 1.9 copy-start.1
  (6 other events, 7.5 us)
Sparse Core Ops, SparseCore 0:
  207.7 115.3 all-reduce.4
  649.5 113.5 all-reduce.6
where the time goes:
time: 900 us; the launch traced here: 896 us
  waiting for transfers between devices  489 us (54%)
  local copies, waits for them, and re-layouts  160 us (18%)
  starting transfers between devices  84.9 us (9%)
  other arithmetic  76.4 us (8%)
  matrix products  65 us (7%)
  between operations  14.5 us (2%)
    psum x1, waiting for transfers between devices, body(): sink_total = lax.psum(sink_sum, 'seq')  112 us
    psum x1, waiting for transfers between devices, spread(): return lax.psum(jnp.where(mine, array, jnp.zeros_like(array)), axis)  109 us
    all_to_all x1, waiting for transfers between devices, body(): lax.all_to_all(flat, 'head', split_axis=0, concat_axis=1, tiled=True)  88.6 us
    all_to_all x1, waiting for transfers between devices, body(): lax.all_to_all(outbound, 'seq', split_axis=0, concat_axis=0, tiled=True)  50.3 us
    all_to_all x1, waiting for transfers between devices, body(): lax.all_to_all(queries, 'head', split_axis=1, concat_axis=0, tiled=True)  45.9 us
    slice x16, local copies, waits for them, and re-layouts, turn(): window_terms = terms[:, SINK_MOST:SINK_MOST + WIN_MOST]  29.9 us
    scatter-add x8, other arithmetic, turn(): placed = jnp.zeros((span + reach, BLK, 2 * width), jnp.float32).at[window...  29.2 us
    all_to_all x1, waiting for transfers between devices, body(): lax.all_to_all(values_wide, 'head', split_axis=1, concat_axis=0, tiled=True)  27.4 us
  transfers between devices with their start and end apart: 12, of which 9 were waited for; matrix products, arithmetic and copies ran while one was open for 6% of the time, Pallas kernels for 0%

commit v1 on v0

--- a/solution.py
+++ b/solution.py
@@ -199,7 +199,7 @@
     arrived = lax.all_to_all(outbound, "seq", split_axis=0, concat_axis=0, tiled=True)
     far_added = jnp.einsum("rcb,rctd->btd", owner_hits, arrived, precision=lax.Precision.HIGHEST)
     spill = shifted(near_sum[:reach], "seq", -1)
-    sink_total = lax.psum(sink_sum, "seq")
+    sink_total = jnp.sum(lax.all_gather(sink_sum, "seq"), axis=0)
     own = near_sum[reach:] + far_added
     own = own + jnp.concatenate(
         [jnp.zeros((local_blocks - reach, BLK, 2 * width), jnp.float32), spill], axis=0

time: 900 us -> 823 us (0.914)
  the two profiles are of different devices: /device:TPU:32 before, /device:TPU:2 now
where the time goes in v1:
time: 823 us; the launch traced here: 819 us
  waiting for transfers between devices  402 us (49%)
  local copies, waits for them, and re-layouts  163 us (20%)
  starting transfers between devices  92.7 us (11%)
  other arithmetic  77 us (9%)
  matrix products  64.2 us (8%)
  between operations  14.6 us (2%)
    psum x1, waiting for transfers between devices, spread(): return lax.psum(jnp.where(mine, array, jnp.zeros_like(array)), axis)  107 us
    all_to_all x1, waiting for transfers between devices, body(): lax.all_to_all(flat, 'head', split_axis=0, concat_axis=1, tiled=True)  92.5 us
    all_to_all x1, waiting for transfers between devices, body(): lax.all_to_all(queries, 'head', split_axis=1, concat_axis=0, tiled=True)  48 us
    all_to_all x1, waiting for transfers between devices, body(): lax.all_to_all(outbound, 'seq', split_axis=0, concat_axis=0, tiled=True)  47.9 us
    slice x16, local copies, waits for them, and re-layouts, turn(): window_terms = terms[:, SINK_MOST:SINK_MOST + WIN_MOST]  30.2 us
    scatter-add x8, other arithmetic, turn(): placed = jnp.zeros((span + reach, BLK, 2 * width), jnp.float32).at[window...  28.9 us
    all_to_all x1, waiting for transfers between devices, body(): lax.all_to_all(values_wide, 'head', split_axis=1, concat_axis=0, tiled=True)  28.2 us
    all_to_all x1, waiting for transfers between devices, body(): lax.all_to_all(keys_wide, 'head', split_axis=1, concat_axis=0, tiled=True)  28.2 us
  transfers between devices with their start and end apart: 12, of which 9 were waited for; matrix products, arithmetic and copies ran while one was open for 8% of the time, Pallas kernels for 0%

profile of v1, /device:TPU:2, one launch (start us, length us, event | category | flops | bytes accessed | tf_op | source)
XLA Modules:
  0.0 819.3 jit_solution(1408217737567059735)
XLA Ops:
  9.0 15.2 %all-to-all-start = ((bf16[128,16,128]{2,0,1:T(8,128)(2,1)}), bf16[128,16,128]{2,0,1:T(8,128)(2,1)S(1)}, u32[]{:S(2)}, u32[]{:S(2)}) async-start(bf16[128,16,128]{2,0,1:T(8,128)(2,1)} %bitcast.5), calls=%async_computation | async-start | bytes 1048576 | tf_op jit(solution)/shard_map/all_to_all | solution.py:67
  25.1 28.2 %all-to-all-done = bf16[128,16,128]{2,0,1:T(8,128)(2,1)S(1)} async-done(((bf16[128,16,128]{2,0,1:T(8,128)(2,1)}), bf16[128,16,128]{2,0,1:T(8,128)(2,1)S(1)}, u32[]{:S(2)}, u32[]{:S(2)}) %all-to-all-start) | async-done | bytes 524320 | tf_op jit(solution)/shard_map/all_to_all | solution.py:67
  54.2 6.3 all-to-all-start.1
  61.4 28.2 %all-to-all-done.1 = bf16[128,16,128]{2,0,1:T(8,128)(2,1)S(1)} async-done(((bf16[128,16,128]{2,0,1:T(8,128)(2,1)}), bf16[128,16,128]{2,0,1:T(8,128)(2,1)S(1)}, u32[]{:S(2)}, u32[]{:S(2)}) %all-to-all-start.1) | async-done | bytes 524320 | tf_op jit(solution)/shard_map/all_to_all | solution.py:68
  89.8 2.0 gather_fusion.1
  91.8 7.6 all-to-all-start.2
  100.8 21.8 %all-to-all-done.2 = bf16[16,2,128,256]{3,2,1,0:T(8,128)(2,1)} async-done(((bf16[16,2,128,256]{3,2,1,0:T(8,128)(2,1)}), bf16[16,2,128,256]{3,2,1,0:T(8,128)(2,1)}, u32[]{:S(2)}, u32[]{:S(2)}) %all-to-all-start.2) | async-done | bytes 2097184 | tf_op jit(solution)/shard_map/all_to_all | solution.py:102
  122.6 10.4 %all-to-all-start.3 = ((bf16[128,32,128]{2,0,1:T(8,128)(2,1)}), bf16[128,32,128]{2,0,1:T(8,128)(2,1)}, u32[]{:S(2)}, u32[]{:S(2)}) async-start(bf16[128,32,128]{2,0,1:T(8,128)(2,1)} %copy.110), calls=%async_computation.3 | async-start | bytes 2097152 | tf_op jit(solution)/shard_map/all_to_all | solution.py:66
  134.5 48.0 %all-to-all-done.3 = bf16[128,32,128]{2,0,1:T(8,128)(2,1)} async-done(((bf16[128,32,128]{2,0,1:T(8,128)(2,1)}), bf16[128,32,128]{2,0,1:T(8,128)(2,1)}, u32[]{:S(2)}, u32[]{:S(2)}) %all-to-all-start.3) | async-done | bytes 1048608 | tf_op jit(solution)/shard_map/all_to_all | solution.py:66
  182.4 8.0 all-to-all-start.4
  195.7 4.6 broadcast_and_fusion
  201.0 4.6 collective-permute-start
  205.9 5.3 collective-permute-done
  211.4 3.3 gather_fusion.2
  214.6 106.8 %all-reduce.4.cloned.1.call-done = bf16[384,256]{1,0:T(8,128)(2,1)} async-done(((bf16[384,256]{1,0:T(8,128)(2,1)}), bf16[384,256]{1,0:T(8,128)(2,1)}) %all-reduce.4.cloned.1.call-update) | async-done | bytes 196624 | tf_op jit(solution)/shard_map/psum | solution.py:15
  323.2 232.7 %while.19 = (s32[]{:T(128)}, f32[19,128,256]{2,1,0:T(8,128)}, f32[3,128,256]{1,0,2:T(4,128)}, bf16[8,2,128,2,128]{4,2,1,0,3:T(8,128)(2,1)}, f32[8,2,1,128,256]{3...) while((s32[]{:T(128)}, f32[19,128,256]{2,1,0:T(8,128)}, ...), condition=%wide.region_9.10_spmd.clone.clone.clone, body=%wide.region_3.9_spmd.sunk.clone.clone.clone.sunk | while | flops 680951808 | bytes 64059104 | solution.py:183
  335.6 2.5 copy.158
  338.1 2.0 constant_dynamic-slice_fusion.6
  340.1 3.6 scatter_fusion
  347.7 2.1 select_add_fusion.2
  364.5 2.5 copy.158
  367.1 2.0 constant_dynamic-slice_fusion.6
  369.1 3.6 scatter_fusion
  372.7 2.0 constant_dynamic-update-slice_fusion.6
  376.7 2.3 select_add_fusion.2
  393.7 2.5 copy.158
  396.2 2.0 constant_dynamic-slice_fusion.6
  398.2 3.6 scatter_fusion
  401.8 2.0 constant_dynamic-update-slice_fusion.6
  405.8 2.3 select_add_fusion.2
  422.8 2.5 copy.158
  425.3 2.0 constant_dynamic-slice_fusion.6
  427.3 3.6 scatter_fusion
  430.9 2.0 constant_dynamic-update-slice_fusion.6
  434.9 2.3 select_add_fusion.2
  451.9 2.5 copy.158
  456.4 3.6 scatter_fusion
  460.0 2.0 constant_dynamic-update-slice_fusion.6
  464.0 2.3 select_add_fusion.2
  481.0 2.5 copy.158
  485.5 3.6 scatter_fusion
  489.1 2.0 constant_dynamic-update-slice_fusion.6
  493.1 2.3 select_add_fusion.2
  510.1 2.5 copy.158
  514.6 3.6 scatter_fusion
  518.2 2.0 constant_dynamic-update-slice_fusion.6
  522.2 2.3 select_add_fusion.2
  539.2 2.5 copy.158
  543.7 3.6 scatter_fusion
  547.3 2.0 constant_dynamic-update-slice_fusion.6
  551.3 2.3 select_add_fusion.2
  558.6 2.2 copy.117
  562.6 5.3 copy.118
  567.9 6.1 all-to-all-start.6
  574.1 9.5 %copy.113 = bf16[2048,2,128]{2,1,0:T(2,128)(2,1)} copy(bf16[2048,2,128]{2,0,1:T(8,128)(2,1)S(1)} %bitcast.246) | data formatting | bytes 2097152 | tf_op jit(solution)/shard_map/reshape | solution.py:184
  583.5 47.9 %all-to-all-done.6 = f32[16,2,128,256]{3,1,2,0:T(2,128)} async-done(((f32[16,2,128,256]{3,1,2,0:T(2,128)}), f32[16,2,128,256]{3,1,2,0:T(2,128)}, u32[]{:S(2)}, u32[]{:S(2)}) %all-to-all-start.6) | async-done | bytes 4194336 | tf_op jit(solution)/shard_map/all_to_all | solution.py:199
  631.4 12.3 %all-to-all-start.5 = ((bf16[2048,2,128]{2,1,0:T(2,128)(2,1)}), bf16[2048,2,128]{2,1,0:T(2,128)(2,1)}, u32[]{:S(2)}, u32[]{:S(2)}) async-start(bf16[2048,2,128]{2,1,0:T(2,128)(2,1)} %copy.113), calls=%async_computation.5 | async-start | bytes 2097152 | tf_op jit(solution)/shard_map/all_to_all | solution.py:185
  648.0 9.6 %collective-permute-start.1 = (f32[3,128,256]{2,0,1:T(4,128)}, f32[3,128,256]{2,0,1:T(4,128)}, u32[]{:S(2)}, u32[]{:S(2)}) collective-permute-start(f32[3,128,256]{2,0,1:T(4,128)} %slice.73), channel_id=1, source_target_pairs={{16,0},{32,16},{48,32},{64,48},{80,64},{96,80},{112,96},{128,112},... | collective-permute-start | bytes 1179656 | tf_op jit(solution)/shard_map/ppermute | solution.py:21
  657.7 23.2 %all-gather.3.cloned.1.call-done = f32[48,128,256]{2,1,0:T(8,128)} async-done(((f32[3,128,256]{2,1,0:T(8,128)}), f32[48,128,256]{2,1,0:T(8,128)}) %all-gather.3.cloned.1.call-update) | async-done | bytes 6291472 | tf_op jit(solution)/shard_map/all_gather | solution.py:202
  680.9 3.4 reduce_sum.68
  684.7 6.7 fusion.25
  692.6 10.0 %copy.124 = f32[2048,1,256]{2,1,0:T(1,128)} copy(f32[2048,1,256]{2,0,1:T(8,128)S(1)} %bitcast.232) | data formatting | bytes 4194304 | tf_op jit(solution)/shard_map/reshape | solution.py:211
  702.6 12.3 %all-to-all-start.7 = ((f32[2048,1,256]{2,1,0:T(1,128)}), f32[2048,1,256]{2,1,0:T(1,128)S(1)}, u32[]{:S(2)}, u32[]{:S(2)}) async-start(f32[2048,1,256]{2,1,0:T(1,128)} %copy.124), calls=%async_computation.7 | async-start | bytes 4194304 | tf_op jit(solution)/shard_map/all_to_all | solution.py:212
  718.0 92.5 %all-to-all-done.7 = f32[2048,1,256]{2,1,0:T(1,128)S(1)} async-done(((f32[2048,1,256]{2,1,0:T(1,128)}), f32[2048,1,256]{2,1,0:T(1,128)S(1)}, u32[]{:S(2)}, u32[]{:S(2)}) %all-to-all-start.7) | async-done | bytes 2097184 | tf_op jit(solution)/shard_map/all_to_all | solution.py:212
  (381 shorter events, 167.6 us)
Async XLA Ops:
  7.2 53.4 %copy-start = (s32[4,256,1]{1,2,0:T(1,128)S(1)}, s32[4,256,1]{1,2,0:T(1,128)}, u32[]{:S(2)}) copy-start(s32[4,256,1]{1,2,0:T(1,128)} %param.16) | copy-start | bytes 12292
  9.0 44.3 %all-to-all-start = ((bf16[128,16,128]{2,0,1:T(8,128)(2,1)}), bf16[128,16,128]{2,0,1:T(8,128)(2,1)S(1)}, u32[]{:S(2)}, u32[]{:S(2)}) async-start(bf16[128,16,128]{2,0,1:T(8,128)(2,1)} %bitcast.5), calls=%async_computation | async-start | bytes 1048576 | tf_op jit(solution)/shard_map/all_to_all | solution.py:67
  54.2 35.4 %all-to-all-start.1 = ((bf16[128,16,128]{2,0,1:T(8,128)(2,1)}), bf16[128,16,128]{2,0,1:T(8,128)(2,1)S(1)}, u32[]{:S(2)}, u32[]{:S(2)}) async-start(bf16[128,16,128]{2,0,1:T(8,128)(2,1)} %bitcast.9), calls=%async_computation.1 | async-start | bytes 1048576 | tf_op jit(solution)/shard_map/all_to_all | solution.py:68
  61.1 144.5 %copy-start.13 = (s32[16,16]{1,0:T(8,128)}, s32[16,16]{1,0:T(8,128)S(1)}, u32[]{:S(2)}) copy-start(s32[16,16]{1,0:T(8,128)S(1)} %convert_reduce_fusion) | copy-start | bytes 3076
  61.2 30.5 %copy-start.17 = (s32[16,2]{0,1:T(2,128)}, s32[16,2]{0,1:T(2,128)S(1)}, u32[]{:S(2)}) copy-start(s32[16,2]{0,1:T(2,128)S(1)} %select_reduce_fusion) | copy-start | bytes 388
  91.8 7.6 copy-start.9
  91.8 30.8 %all-to-all-start.2 = ((bf16[16,2,128,256]{3,2,1,0:T(8,128)(2,1)}), bf16[16,2,128,256]{3,2,1,0:T(8,128)(2,1)}, u32[]{:S(2)}, u32[]{:S(2)}) async-start(bf16[16,2,128,256]{3,2,1,0:T(8,128)(2,1)} %bitcast.19), calls=%async_computation.2 | async-start | bytes 4194304 | tf_op jit(solution)/shard_map/all_to_all | solution.py:102
  99.4 33.6 %copy-start.10 = (bf16[128,32,128]{2,1,0:T(8,128)(2,1)S(1)}, bf16[128,32,128]{2,1,0:T(8,128)(2,1)}, u32[]{:S(2)}) copy-start(bf16[128,32,128]{2,1,0:T(8,128)(2,1)} %param.15) | copy-start | bytes 3145732
  122.6 59.8 %all-to-all-start.3 = ((bf16[128,32,128]{2,0,1:T(8,128)(2,1)}), bf16[128,32,128]{2,0,1:T(8,128)(2,1)}, u32[]{:S(2)}, u32[]{:S(2)}) async-start(bf16[128,32,128]{2,0,1:T(8,128)(2,1)} %copy.110), calls=%async_computation.3 | async-start | bytes 2097152 | tf_op jit(solution)/shard_map/all_to_all | solution.py:66
  133.0 57.5 %copy-start.19 = (s32[4]{0:T(128)S(1)}, s32[4]{0:T(128)}, u32[]{:S(2)}) copy-start(s32[4]{0:T(128)} %param.17) | copy-start | bytes 52
  133.1 58.1 %copy-start.20 = (s32[4]{0:T(128)S(1)}, s32[4]{0:T(128)}, u32[]{:S(2)}) copy-start(s32[4]{0:T(128)} %param.18) | copy-start | bytes 52
  182.4 139.0 %all-to-all-start.4 = ((bf16[128,32,128]{2,0,1:T(8,128)(2,1)}), bf16[128,32,128]{2,0,1:T(8,128)(2,1)}, u32[]{:S(2)}, u32[]{:S(2)}) async-start(bf16[128,32,128]{2,0,1:T(8,128)(2,1)} %copy.111), calls=%async_computation.4 | async-start | bytes 2097152 | tf_op jit(solution)/shard_map/all_to_all | solution.py:69
  190.5 131.0 %all-reduce.4.cloned.1.call-start = ((), (), s32[]{:S(2)}) async-start(), calls=%async_computation.8 | async-start | bytes 393216 | tf_op jit(solution)/shard_map/psum | solution.py:15
  201.0 10.2 %collective-permute-start = (bf16[384,256]{1,0:T(8,128)(2,1)S(1)}, bf16[384,256]{1,0:T(8,128)(2,1)S(1)}, u32[]{:S(2)}, u32[]{:S(2)}) collective-permute-start(bf16[384,256]{1,0:T(8,128)(2,1)S(1)} %get-tuple-element.239), channel_id=1, source_target_pairs={{0,16},{16,32},{32,48},{48,64},{64,80},{80,96},{96,112},{112,128},... | collective-permute-start | bytes 589832 | tf_op jit(solution)/shard_map/ppermute | solution.py:21
  205.7 475.2 %all-gather.3.cloned.1.call-start = ((), (), s32[]{:S(2)}) async-start(), calls=%async_computation.9 | async-start | bytes 6684672 | tf_op jit(solution)/shard_map/all_gather | solution.py:202
  211.4 111.8 %copy-start.12 = (s32[8]{0:T(128)S(1)}, s32[8]{0:T(128)}, u32[]{:S(2)}) copy-start(s32[8]{0:T(128)} %constant.226) | copy-start | bytes 100
  321.5 1.7 copy-start.8
  323.2 1.3 copy-start.21
  323.2 3.0 copy-start.6
  326.2 2.9 copy-start.2
  347.7 4.4 copy-start.7
  347.7 4.4 copy-start.22
  352.1 1.3 copy-start.21
  352.1 3.0 copy-start.6
  355.2 2.9 copy-start.2
  376.7 4.5 copy-start.7
  376.7 4.5 copy-start.22
  381.2 1.3 copy-start.21
  381.2 3.0 copy-start.6
  384.3 2.9 copy-start.2
  405.8 4.5 copy-start.7
  405.8 4.5 copy-start.22
  410.3 3.0 copy-start.6
  413.4 2.9 copy-start.2
  434.9 4.5 copy-start.7
  434.9 4.5 copy-start.22
  439.4 3.0 copy-start.6
  442.5 2.9 copy-start.2
  464.0 4.5 copy-start.7
  464.0 4.5 copy-start.22
  468.5 3.0 copy-start.6
  471.6 2.9 copy-start.2
  493.1 4.5 copy-start.7
  493.1 4.5 copy-start.22
  497.6 3.0 copy-start.6
  500.7 2.9 copy-start.2
  522.2 4.5 copy-start.7
  522.2 4.5 copy-start.22
  526.8 3.0 copy-start.6
  529.8 2.9 copy-start.2
  551.3 4.5 copy-start.7
  551.3 4.5 copy-start.22
  567.9 6.1 copy-start.11
  567.9 63.5 %all-to-all-start.6 = ((f32[16,2,128,256]{3,1,2,0:T(2,128)}), f32[16,2,128,256]{3,1,2,0:T(2,128)}, u32[]{:S(2)}, u32[]{:S(2)}) async-start(f32[16,2,128,256]{3,1,2,0:T(2,128)} %copy.118), calls=%async_computation.6 | async-start | bytes 8388608 | tf_op jit(solution)/shard_map/all_to_all | solution.py:199
  574.0 69.8 %copy-start.3 = (f32[19,128,256]{2,1,0:T(8,128)S(1)}, f32[19,128,256]{2,1,0:T(8,128)}, u32[]{:S(2)}) copy-start(f32[19,128,256]{2,1,0:T(8,128)} %get-tuple-element.84) | copy-start | bytes 7471108
  631.4 71.2 %all-to-all-start.5 = ((bf16[2048,2,128]{2,1,0:T(2,128)(2,1)}), bf16[2048,2,128]{2,1,0:T(2,128)(2,1)}, u32[]{:S(2)}, u32[]{:S(2)}) async-start(bf16[2048,2,128]{2,1,0:T(2,128)(2,1)} %copy.113), calls=%async_computation.5 | async-start | bytes 2097152 | tf_op jit(solution)/shard_map/all_to_all | solution.py:185
  643.8 13.8 %copy-start.14 = (s32[16,16]{1,0:T(8,128)S(1)}, s32[16,16]{1,0:T(8,128)}, u32[]{:S(2)}) copy-start(s32[16,16]{1,0:T(8,128)} %copy-done.13) | copy-start | bytes 3076
  643.8 13.8 %copy-start.16 = (pred[16,16]{1,0:T(8,128)(4,1)S(1)}, pred[16,16]{1,0:T(8,128)(4,1)}, u32[]{:S(2)}) copy-start(pred[16,16]{1,0:T(8,128)(4,1)} %copy-done.15) | copy-start | bytes 772
  645.3 1.8 copy-start.4
  648.0 36.7 %collective-permute-start.1 = (f32[3,128,256]{2,0,1:T(4,128)}, f32[3,128,256]{2,0,1:T(4,128)}, u32[]{:S(2)}, u32[]{:S(2)}) collective-permute-start(f32[3,128,256]{2,0,1:T(4,128)} %slice.73), channel_id=1, source_target_pairs={{16,0},{32,16},{48,32},{64,48},{80,64},{96,80},{112,96},{128,112},... | collective-permute-start | bytes 1179656 | tf_op jit(solution)/shard_map/ppermute | solution.py:21
  680.9 3.8 copy-start.5
  680.9 3.8 copy-start.18
  702.6 107.9 %all-to-all-start.7 = ((f32[2048,1,256]{2,1,0:T(1,128)}), f32[2048,1,256]{2,1,0:T(1,128)S(1)}, u32[]{:S(2)}, u32[]{:S(2)}) async-start(f32[2048,1,256]{2,1,0:T(1,128)} %copy.124), calls=%async_computation.7 | async-start | bytes 4194304 | tf_op jit(solution)/shard_map/all_to_all | solution.py:212
  810.5 1.9 copy-start.1
  (6 other events, 7.4 us)
Sparse Core Ops, SparseCore 0:
  205.8 115.5 all-reduce.3
  558.0 122.8 all-gather.2
